TPU v7x, 32 devices: a whole 2x2x4 slice. The times are simulated.
32 devices in a mesh: seq: 8 (over z, y), tensor: 4 (over x, core).
Axes of the slice: x: 2, y: 2, z: 4, core: 2. Of those that a mesh axis runs over, the one named last changes fastest.
Arguments:
- query: bfloat16 [1024, 2048], P('seq', 'tensor')
- suffix_kv: bfloat16 [1024, 4, 2, 128], P('seq'), may hold values from -6 to 6
- segment_ids: int32 [8, 128], P('seq'), may hold values from 0 to 3, never falling along the last dimension, each value on 1 to 64 neighbouring positions
- request_prefix: int32 [8, 4], P('seq'), may hold values from 0 to 3
- prefix_kv: bfloat16 [8192, 4, 2, 128], P('seq')
- shard_prefix: int32 [8], P('seq'), may hold values from 0 to 3, as said below
- residual: bfloat16 [1024, 2048], P('seq'), may hold values from -3.2 to 3.2
- out_weight: bfloat16 [2048, 2048], P('tensor'), may hold values from -0.1875 to 0.1875
- norm_gain: float32 [2048], replicated, may hold values from 0.1 to 1.9
- expert_ids: int32 [1024, 6], P('seq'), may hold values from 0 to 15, all different within a row; in each aligned block of 128 rows (0 to 127, 128 to 255, ...) at most 96 rows name the same one
- gate_weights: float32 [1024, 6], P('seq'), may hold values from 0.05 to 0.5
- expert_in: bfloat16 [16, 2048, 2, 1408], P('seq', None, None, 'tensor'), may hold values from -0.125 to 0.125
- expert_out: bfloat16 [16, 1408, 2048], P('seq', 'tensor'), may hold values from -0.21875 to 0.21875
Outputs:
- attended: bfloat16 [1024, 2048], P('seq', 'tensor')
- layer_out: bfloat16 [1024, 2048], P('seq', 'tensor')
Inputs may be any that keep to these rules, and one draw needn't show every extreme that they name: `segment_ids`: on each seq index the segment numbers never fall along the 128 positions and every number occurs. `shard_prefix`: every prefix owns the same number of shards. `expert_ids`: each row names 6 different experts; within the 128 rows of one seq index no expert is named more than 96 times, and that count is reached.
All inputs are finite; a program needn't handle non-finite values.
Results may differ from a plain program's by a relative error of at most 0.02.
Values may be sent and summed in bfloat16 or wider, within the bound.
A program may use at most 128 MiB of HBM per device.

v0:
```python
import jax
import jax.numpy as jnp
from jax import lax
from jax.sharding import PartitionSpec as P

QH = 16
KVH = 4


NEG_FLOOR = -1e30


def fold_block(carried, queries, key_rows, values, allowed, score_scale):
    running_max, running_sum, weighted = carried
    scores = (
        jnp.einsum("rhd,kd->rhk", queries, key_rows, preferred_element_type=jnp.float32)
        * score_scale
    )
    scores = jnp.where(allowed[:, None, :], scores, -jnp.inf)
    new_max = jnp.maximum(running_max, jnp.max(scores, axis=2))
    weights = jnp.exp(scores - new_max[:, :, None])
    shrink = jnp.exp(running_max - new_max)
    gathered = jnp.einsum(
        "rhk,kd->rhd", weights.astype(jnp.bfloat16), values, preferred_element_type=jnp.float32
    )
    return (
        new_max,
        running_sum * shrink + jnp.sum(weights, axis=2),
        weighted * shrink[:, :, None] + gathered,
    )


def body(
    query,
    suffix_kv,
    segment_ids,
    request_prefix,
    prefix_kv,
    shard_prefix,
    residual,
    out_weight,
    norm_gain,
    expert_ids,
    gate_weights,
    expert_in,
    expert_out,
):
    tok_rows = query.shape[0]
    head_size = suffix_kv.shape[3]
    heads_here = query.shape[1] // head_size
    kv_head = lax.axis_index("tensor") * heads_here // (QH // KVH)
    score_scale = head_size ** (-0.5)
    queries = query.reshape(tok_rows, heads_here, head_size)
    segments = segment_ids[0]
    requests = jnp.arange(request_prefix.shape[1], dtype=jnp.int32)
    row_prefix = jnp.sum(
        jnp.where(segments[:, None] == requests[None, :], request_prefix[0][None, :], 0), axis=1
    )
    blank_state = (
        jnp.full((tok_rows, heads_here), NEG_FLOOR, jnp.float32),
        jnp.zeros((tok_rows, heads_here), jnp.float32),
        jnp.zeros((tok_rows, heads_here, head_size), jnp.float32),
    )
    shard_len = prefix_kv.shape[0]
    own_cache = lax.dynamic_slice_in_dim(prefix_kv, kv_head, 1, 1).reshape(shard_len, 2 * head_size)
    cache_rows = lax.all_gather(own_cache, "seq", axis=0, tiled=True)
    owners = lax.all_gather(shard_prefix, "seq", axis=0, tiled=True)
    shard_count = owners.shape[0]
    shards = cache_rows.reshape(shard_count, -1, 2, head_size)

    def one_shard(inner_state, shard_item):
        block_rows, shard_owner = shard_item
        matching = row_prefix == shard_owner

        def attend(current):
            allowed = jnp.broadcast_to(matching[:, None], (tok_rows, block_rows.shape[0]))
            return fold_block(
                current, queries, block_rows[:, 0], block_rows[:, 1], allowed, score_scale
            )

        return (lax.cond(jnp.any(matching), attend, lambda current: current, inner_state), None)

    final_state, unused = lax.scan(one_shard, blank_state, (shards, owners))
    carried = final_state
    own_suffix = lax.dynamic_slice_in_dim(suffix_kv, kv_head, 1, 1).reshape(tok_rows, 2, head_size)
    positions = jnp.arange(tok_rows)
    causal = (segments[:, None] == segments[None, :]) & (positions[None, :] <= positions[:, None])
    carried = fold_block(carried, queries, own_suffix[:, 0], own_suffix[:, 1], causal, score_scale)
    running_max, running_sum, weighted = carried
    attention = (
        (weighted / running_sum[:, :, None])
        .reshape(tok_rows, heads_here * head_size)
        .astype(jnp.bfloat16)
    )
    projected = jnp.dot(attention, out_weight, preferred_element_type=jnp.float32)
    model_width = residual.shape[1]
    slice_width = model_width // lax.axis_size("tensor")
    first_col = lax.axis_index("tensor") * slice_width
    shared = lax.psum_scatter(projected, "tensor", scatter_dimension=1, tiled=True)
    hidden_state = (
        lax.dynamic_slice_in_dim(residual, first_col, slice_width, 1).astype(jnp.float32) + shared
    )
    squares = lax.psum(jnp.sum(hidden_state * hidden_state, axis=1), "tensor")
    gain_cols = lax.dynamic_slice_in_dim(norm_gain, first_col, slice_width, 0)
    normed = (
        hidden_state * lax.rsqrt(squares / model_width + 1e-06)[:, None] * gain_cols[None, :]
    ).astype(jnp.bfloat16)
    attended = hidden_state.astype(jnp.bfloat16)
    exp_here = expert_in.shape[0]
    sources = lax.axis_size("seq")
    experts = exp_here * sources
    top_k = expert_ids.shape[1]
    capacity = 2 * tok_rows * top_k // experts
    flat_ids = expert_ids.reshape(-1)
    onehot = (flat_ids[:, None] == jnp.arange(experts, dtype=jnp.int32)[None, :]).astype(jnp.int32)
    slot_index = jnp.sum((jnp.cumsum(onehot, axis=0) - 1) * onehot, axis=1)
    places = flat_ids * capacity + slot_index
    outgoing = (
        jnp.zeros((experts * capacity, slice_width), jnp.bfloat16)
        .at[places]
        .set(jnp.repeat(normed, top_k, axis=0))
    )
    incoming = lax.all_to_all(
        outgoing.reshape(sources, exp_here, capacity, slice_width),
        "seq",
        split_axis=0,
        concat_axis=0,
        tiled=True,
    )
    gate_up = jnp.einsum(
        "sjcd,jdgh->sjcgh",
        lax.all_gather(incoming, "tensor", axis=3, tiled=True),
        expert_in,
        preferred_element_type=jnp.float32,
    )
    hidden = (jax.nn.silu(gate_up[:, :, :, 0]) * gate_up[:, :, :, 1]).astype(jnp.bfloat16)
    group_terms = jnp.einsum(
        "sjch,jhd->sjcd", hidden, expert_out, preferred_element_type=jnp.float32
    )
    expert_rows_out = lax.psum_scatter(
        group_terms.astype(jnp.bfloat16), "tensor", scatter_dimension=3, tiled=True
    )
    returned = lax.all_to_all(expert_rows_out, "seq", split_axis=0, concat_axis=0, tiled=True)
    picked = returned.reshape(experts * capacity, slice_width)[places].reshape(
        tok_rows, top_k, slice_width
    )
    mixture = jnp.sum(gate_weights[:, :, None] * picked.astype(jnp.float32), axis=1)
    layer_out = (hidden_state + mixture).astype(jnp.bfloat16)
    return (attended, layer_out)


def solution(mesh):
    in_specs = (
        P("seq", "tensor"),
        P("seq", None, None, None),
        P("seq", None),
        P("seq", None),
        P("seq", None, None, None),
        P("seq"),
        P("seq", None),
        P("tensor", None),
        P(),
        P("seq", None),
        P("seq", None),
        P("seq", None, None, "tensor"),
        P("seq", "tensor", None),
    )
    out_specs = (P("seq", "tensor"), P("seq", "tensor"))
    return jax.shard_map(body, mesh=mesh, in_specs=in_specs, out_specs=out_specs, check_vma=False)
```

profile of v0, /device:TPU:0, one launch (start us, length us, event | category | flops | bytes accessed | tf_op | source)
XLA Modules:
  0.0 414.1 jit_solution(4523688485065181562)
XLA Ops:
  7.3 1.6 constant_dynamic-slice_fusion.1
  8.8 1.1 copy.101
  11.3 0.8 dynamic-update-slice
  12.1 13.2 %all-reduce = s32[8]{0:T(128)S(1)} all-reduce(s32[8]{0:T(128)S(1)} %dynamic-update-slice), channel_id=1, replica_groups=mesh['seq'=8,'tensor'=4] {'seq'}, use_global_device_ids=true, to_apply=%add | all-reduce | flops 8 | bytes 64
  25.5 0.9 constant_dynamic-slice_fusion
  26.8 59.6 %all-gather.3.cloned.1.call-done = bf16[8192,256]{0,1:T(8,128)(2,1)} async-done(((bf16[1024,256]{0,1:T(8,128)(2,1)}), bf16[8192,256]{0,1:T(8,128)(2,1)}) %all-gather.3.cloned.1.call-update) | async-done | bytes 4194320 | tf_op jit(solution)/shard_map/all_gather | solution.py:66
  86.4 8.5 %copy.104 = bf16[32,8,8,1024]{3,2,1,0:T(8,128)(2,1)} copy(bf16[32,8,8,1024]{3,1,2,0:T(8,128)(2,1)} %bitcast.115) | data formatting | bytes 8388608
  94.9 6.6 %copy.78 = bf16[8,1024,2,128]{3,1,2,0:T(8,128)(2,1)} copy(bf16[8,1024,2,128]{1,0,3,2:T(8,128)(2,1)} %bitcast.113) | data formatting | bytes 8388608 | tf_op jit(solution)/shard_map/while | solution.py:83
  101.5 0.7 broadcast_in_dim.76
  102.2 39.8 %while.14 = (s32[]{:T(128)}, f32[128,4]{0,1:T(4,128)S(1)}, f32[128,4]{0,1:T(4,128)S(1)}, f32[128,4,128]{2,0,1:T(8,128)}, s32[8]{0:T(128)S(1)}, /*index=5*/s32[12...) while((s32[]{:T(128)}, f32[128,4]{0,1:T(4,128)S(1)}, ...), condition=%wide.region_7.8_spmd, body=%wide.region_1.7_spmd.sunk | while | flops 274334976 | bytes 10651679 | solution.py:83
  102.8 1.3 fusion.48
  105.3 1.3 fusion.48
  107.8 1.3 fusion.48
  109.6 3.4 conditional.2
  109.6 1.1 dynamic-slice_bitcast_fusion
  111.7 0.6 convolution_add_fusion
  112.3 0.7 copy-done.3
  113.6 1.3 fusion.48
  115.4 3.4 conditional.2
  115.4 1.1 dynamic-slice_bitcast_fusion
  117.5 0.6 convolution_add_fusion
  118.1 0.7 copy-done.3
  119.4 1.3 fusion.48
  121.2 3.4 conditional.2
  121.2 1.1 dynamic-slice_bitcast_fusion
  123.9 0.7 copy-done.3
  125.2 1.3 fusion.48
  127.0 3.4 conditional.2
  127.0 1.1 dynamic-slice_bitcast_fusion
  129.7 0.7 copy-done.3
  131.0 1.3 fusion.48
  132.8 3.4 conditional.2
  132.8 1.1 dynamic-slice_bitcast_fusion
  134.9 0.6 convolution_add_fusion
  135.5 0.7 copy-done.3
  136.8 1.3 fusion.48
  138.6 3.4 conditional.2
  138.6 1.1 dynamic-slice_bitcast_fusion
  141.3 0.7 copy-done.3
  142.0 1.8 copy.82
  143.8 1.2 fusion.26
  145.1 3.1 fusion.42
  148.7 1.7 reduce-window.6
  150.9 0.8 dynamic_slice.25
  151.8 19.7 %reduce-scatter.3.cloned.1.call-done = f32[128,512]{1,0:T(8,128)} async-done(((f32[128,2048]{1,0:T(8,128)}), f32[128,512]{1,0:T(8,128)}) %reduce-scatter.3.cloned.1.call-update) | async-done | bytes 262160 | tf_op jit(solution)/shard_map/reduce_scatter | solution.py:99
  171.5 1.1 multiply_reduce_fusion.1
  172.6 5.9 %psum.7 = f32[128]{0:T(128)S(1)} all-reduce(f32[128]{0:T(128)S(1)} %multiply_reduce_fusion.1), channel_id=1, replica_groups=mesh['seq'=8,'tensor'=4] {'tensor'}, use_global_device_ids=true, to_apply=%region_15.16 | all-reduce | flops 128 | bytes 1024 | tf_op jit(solution)/shard_map/psum | solution.py:103
  178.5 1.0 multiply_convert_fusion
  179.6 1.1 broadcast_in_dim.83
  180.7 2.1 reshape.146
  182.8 7.3 %scatter_custom_fusion = bf16[1536,512]{1,0:T(8,128)(2,1)} fusion(s32[768]{0:T(1024)S(1)} %fusion.37, bf16[768,512]{1,0:T(8,128)(2,1)} %reshape.146, bf16[]{:T(256)} %constant.71.clone.1), kind=kCustom, calls=%fused_computation.39 | custom fusion | bytes 1573376 | tf_op jit(solution)/shard_map/scatter | solution.py:121
  190.1 42.5 %all_to_all.10 = bf16[8,2,96,512]{3,2,1,0:T(8,128)(2,1)S(1)} all-to-all(bf16[8,2,96,512]{3,2,1,0:T(8,128)(2,1)} %bitcast.114), channel_id=1, replica_groups=mesh['seq'=8,'tensor'=4] {'seq'}, dimensions={0} | all-to-all | bytes 3145728 | tf_op jit(solution)/shard_map/all_to_all | solution.py:123
  232.6 1.2 copy.90
  234.0 44.6 %all-gather.5.cloned.1.call-done = bf16[8,2,96,2048]{3,2,0,1:T(8,128)(2,1)} async-done(((bf16[8,2,96,512]{3,2,0,1:T(8,128)(2,1)}), bf16[8,2,96,2048]{3,2,0,1:T(8,128)(2,1)}) %all-gather.5.cloned.1.call-update) | async-done | bytes 6291472 | tf_op jit(solution)/shard_map/all_gather | solution.py:132
  278.5 8.1 %fusion.16 = f32[8,2,96,2,352]{4,2,3,0,1:T(8,128)S(1)} fusion(bf16[2,2048,2,352]{1,3,2,0:T(8,128)(2,1)} %param.28, bf16[8,2,96,2048]{3,2,0,1:T(8,128)(2,1)} %all-gather.5.cloned.1.call-done), kind=kOutput, calls=%fused_computation.30 | convolution fusion | flops 4429185024 | bytes 16384000 | tf_op jit(solution)/shard_map/sjcd,jdgh->sjcgh/dot_general | solution.py:130
  286.6 5.4 %convert_bitcast_fusion = bf16[8,2,96,2048]{3,2,0,1:T(8,128)(2,1)} fusion(bf16[2,352,2048]{2,1,0:T(8,128)(2,1)S(1)} %copy-done, f32[8,2,96,2,352]{4,2,3,0,1:T(8,128)S(1)} %fusion.16), kind=kOutput, calls=%fused_computation.23 | convolution fusion | flops 2220982272 | bytes 13500416 | tf_op jit(solution)/shard_map/sjch,jhd->sjcd/dot_general | solution.py:137
  292.1 58.5 %reduce-scatter.5.cloned.1.call-done = bf16[8,2,96,512]{3,2,0,1:T(8,128)(2,1)} async-done(((bf16[8,2,96,2048]{3,2,0,1:T(8,128)(2,1)}), bf16[8,2,96,512]{3,2,0,1:T(8,128)(2,1)}) %reduce-scatter.5.cloned.1.call-update) | async-done | bytes 1572880 | tf_op jit(solution)/shard_map/reduce_scatter | solution.py:140
  350.6 2.7 copy.92
  353.3 5.6 %all-to-all-start.1 = ((bf16[8,2,96,512]{3,2,1,0:T(8,128)(2,1)}), bf16[8,2,96,512]{3,2,1,0:T(8,128)(2,1)}, u32[]{:S(2)}, u32[]{:S(2)}) async-start(bf16[8,2,96,512]{3,2,1,0:T(8,128)(2,1)} %copy.92), calls=%async_computation.3 | async-start | bytes 3145728 | tf_op jit(solution)/shard_map/all_to_all | solution.py:143
  359.1 37.0 %all-to-all-done.1 = bf16[8,2,96,512]{3,2,1,0:T(8,128)(2,1)} async-done(((bf16[8,2,96,512]{3,2,1,0:T(8,128)(2,1)}), bf16[8,2,96,512]{3,2,1,0:T(8,128)(2,1)}, u32[]{:S(2)}, u32[]{:S(2)}) %all-to-all-start.1) | async-done | bytes 1572896 | tf_op jit(solution)/shard_map/all_to_all | solution.py:143
  396.1 5.0 %gather_fusion = bf16[768,512]{1,0:T(8,128)(2,1)} fusion(bf16[1536,512]{1,0:T(8,128)(2,1)} %bitcast.31, s32[1024]{0:T(1024)S(1)} %pad_clamp_fusion), kind=kCustom, calls=%fused_computation | custom fusion | bytes 1575936 | tf_op jit(solution)/shard_map/gather | solution.py:144
  401.0 2.5 reshape.133
  403.6 2.3 multiply_reduce_fusion
  405.9 1.7 add_convert_fusion
  (114 shorter events, 14.9 us)
Async XLA Ops:
  7.2 279.5 %copy-start = (bf16[2,352,2048]{2,1,0:T(8,128)(2,1)S(1)}, bf16[2,352,2048]{2,1,0:T(8,128)(2,1)}, u32[]{:S(2)}) copy-start(bf16[2,352,2048]{2,1,0:T(8,128)(2,1)} %param.29) | copy-start | bytes 8650756
  7.2 3.5 copy-start.10
  7.2 18.0 %copy-start.5 = (bf16[128,512]{1,0:T(8,128)(2,1)S(1)}, bf16[128,512]{1,0:T(8,128)(2,1)}, u32[]{:S(2)}) copy-start(bf16[128,512]{1,0:T(8,128)(2,1)} %param.17) | copy-start | bytes 393220
  7.2 19.2 %copy-start.8 = (s32[1,128]{1,0:T(1,128)S(1)}, s32[1,128]{1,0:T(1,128)}, u32[]{:S(2)}) copy-start(s32[1,128]{1,0:T(1,128)} %param.19) | copy-start | bytes 1540
  7.2 19.2 %copy-start.9 = (s32[1,4]{1,0:T(1,128)S(1)}, s32[1,4]{1,0:T(1,128)}, u32[]{:S(2)}) copy-start(s32[1,4]{1,0:T(1,128)} %param.20) | copy-start | bytes 52
  7.2 79.2 %all-gather.3.cloned.1.call-start = ((), (), s32[]{:S(2)}) async-start(), calls=%async_computation.4 | async-start | bytes 4718592 | tf_op jit(solution)/shard_map/all_gather | solution.py:66
  10.0 161.5 %reduce-scatter.3.cloned.1.call-start = ((), (), s32[]{:S(2)}) async-start(), calls=%async_computation.5 | async-start | bytes 1310720 | tf_op jit(solution)/shard_map/reduce_scatter | solution.py:99
  110.7 1.0 copy-start.2
  112.3 0.7 copy-start.3
  116.5 1.0 copy-start.2
  118.1 0.7 copy-start.3
  122.3 1.0 copy-start.2
  123.9 0.7 copy-start.3
  128.1 1.0 copy-start.2
  129.7 0.7 copy-start.3
  133.9 1.0 copy-start.2
  135.5 0.7 copy-start.3
  139.7 1.0 copy-start.2
  141.3 0.7 copy-start.3
  145.0 3.2 copy-start.6
  145.0 26.5 %copy-start.4 = (bf16[128,2048]{1,0:T(8,128)(2,1)S(1)}, bf16[128,2048]{1,0:T(8,128)(2,1)}, u32[]{:S(2)}) copy-start(bf16[128,2048]{1,0:T(8,128)(2,1)} %param.23) | copy-start | bytes 1572868
  148.2 130.3 %all-gather.5.cloned.1.call-start = ((), (), s32[]{:S(2)}) async-start(), calls=%async_computation.6 | async-start | bytes 7864320 | tf_op jit(solution)/shard_map/all_gather | solution.py:132
  233.9 116.7 %reduce-scatter.5.cloned.1.call-start = ((), (), s32[]{:S(2)}) async-start(), calls=%async_computation.7 | async-start | bytes 7864320 | tf_op jit(solution)/shard_map/reduce_scatter | solution.py:140
  353.3 5.7 %copy-start.7 = (f32[128,6]{0,1:T(8,128)S(1)}, f32[128,6]{0,1:T(8,128)}, u32[]{:S(2)}) copy-start(f32[128,6]{0,1:T(8,128)} %param.27) | copy-start | bytes 9220
  353.3 42.8 %all-to-all-start.1 = ((bf16[8,2,96,512]{3,2,1,0:T(8,128)(2,1)}), bf16[8,2,96,512]{3,2,1,0:T(8,128)(2,1)}, u32[]{:S(2)}, u32[]{:S(2)}) async-start(bf16[8,2,96,512]{3,2,1,0:T(8,128)(2,1)} %copy.92), calls=%async_computation.3 | async-start | bytes 3145728 | tf_op jit(solution)/shard_map/all_to_all | solution.py:143
  401.0 4.9 %copy-start.1 = (f32[128,512]{1,0:T(8,128)S(1)}, f32[128,512]{1,0:T(8,128)}, u32[]{:S(2)}) copy-start(f32[128,512]{1,0:T(8,128)} %reduce-scatter.3.cloned.1.call-done) | copy-start | bytes 786436
Sparse Core Ops, SparseCore 0:
  10.2 76.0 all-gather.2
  148.3 23.1 reduce-scatter.2
  234.0 44.4 all-gather.4
  292.2 58.3 reduce-scatter.4
where the time goes:
time: 418 us; the launch traced here: 414 us
  waiting for transfers between devices  219 us (52%)
  local copies, waits for them, and re-layouts  62.1 us (15%)
  blocking collectives  61.6 us (15%)
  matrix products  24.3 us (6%)
  other arithmetic  21.2 us (5%)
  between operations  14.7 us (4%)
  starting transfers between devices  5.81 us (1%)
  loops' own time  5.05 us (1%)
    all_gather x1, waiting for transfers between devices, body(): cache_rows = lax.all_gather(own_cache, 'seq', axis=0, tiled=True)  59.6 us
    reduce_scatter x1, waiting for transfers between devices, body(): lax.psum_scatter(group_terms.astype(jnp.bfloat16), 'tensor', scatter_dime...  58.5 us
    all_gather x1, waiting for transfers between devices, body(): lax.all_gather(incoming, 'tensor', axis=3, tiled=True)  44.6 us
    all_to_all x1, blocking collectives, body(): lax.all_to_all(outgoing.reshape(sources, exp_here, capacity, slice_width)...  42.5 us
    all_to_all x1, waiting for transfers between devices, body(): lax.all_to_all(expert_rows_out, 'seq', split_axis=0, concat_axis=0, tiled...  37 us
    reduce_scatter x1, waiting for transfers between devices, body(): lax.psum_scatter(projected, 'tensor', scatter_dimension=1, tiled=True)  19.7 us
    unnamed x1, blocking collectives  13.2 us
    unnamed x26, local copies, waits for them, and re-layouts  11.3 us
  transfers between devices with their start and end apart: 5, of which 5 were waited for; matrix products, arithmetic and copies ran while one was open for 2% of the time, Pallas kernels for 0%

commit v1 on v0

--- a/solution.py
+++ b/solution.py
@@ -96,10 +96,12 @@
     model_width = residual.shape[1]
     slice_width = model_width // lax.axis_size("tensor")
     first_col = lax.axis_index("tensor") * slice_width
-    shared = lax.psum_scatter(projected, "tensor", scatter_dimension=1, tiled=True)
-    hidden_state = (
-        lax.dynamic_slice_in_dim(residual, first_col, slice_width, 1).astype(jnp.float32) + shared
+    shared = lax.psum_scatter(
+        projected.astype(jnp.bfloat16), "tensor", scatter_dimension=1, tiled=True
     )
+    hidden_state = lax.dynamic_slice_in_dim(residual, first_col, slice_width, 1).astype(
+        jnp.float32
+    ) + shared.astype(jnp.float32)
     squares = lax.psum(jnp.sum(hidden_state * hidden_state, axis=1), "tensor")
     gain_cols = lax.dynamic_slice_in_dim(norm_gain, first_col, slice_width, 0)
     normed = (
@@ -107,45 +109,26 @@
     ).astype(jnp.bfloat16)
     attended = hidden_state.astype(jnp.bfloat16)
     exp_here = expert_in.shape[0]
-    sources = lax.axis_size("seq")
-    experts = exp_here * sources
-    top_k = expert_ids.shape[1]
-    capacity = 2 * tok_rows * top_k // experts
-    flat_ids = expert_ids.reshape(-1)
-    onehot = (flat_ids[:, None] == jnp.arange(experts, dtype=jnp.int32)[None, :]).astype(jnp.int32)
-    slot_index = jnp.sum((jnp.cumsum(onehot, axis=0) - 1) * onehot, axis=1)
-    places = flat_ids * capacity + slot_index
-    outgoing = (
-        jnp.zeros((experts * capacity, slice_width), jnp.bfloat16)
-        .at[places]
-        .set(jnp.repeat(normed, top_k, axis=0))
-    )
-    incoming = lax.all_to_all(
-        outgoing.reshape(sources, exp_here, capacity, slice_width),
-        "seq",
-        split_axis=0,
-        concat_axis=0,
-        tiled=True,
-    )
-    gate_up = jnp.einsum(
-        "sjcd,jdgh->sjcgh",
-        lax.all_gather(incoming, "tensor", axis=3, tiled=True),
-        expert_in,
+    hid = expert_in.shape[3]
+    experts = exp_here * lax.axis_size("seq")
+    named = expert_ids[:, :, None] == jnp.arange(experts, dtype=jnp.int32)[None, None, :]
+    gates = jnp.sum(jnp.where(named, gate_weights[:, :, None], 0.0), axis=1)
+    all_gates = lax.all_gather(gates, "seq", axis=0, tiled=True)
+    own_gates = lax.dynamic_slice_in_dim(all_gates, lax.axis_index("seq") * exp_here, exp_here, 1)
+    rows = lax.all_gather(normed, "seq", axis=0, tiled=True)
+    rows = lax.all_gather(rows, "tensor", axis=1, tiled=True)
+    gate_up = jnp.einsum("rd,jdgh->rjgh", rows, expert_in, preferred_element_type=jnp.float32)
+    hidden = jax.nn.silu(gate_up[:, :, 0]) * gate_up[:, :, 1] * own_gates[:, :, None]
+    terms = jnp.dot(
+        hidden.astype(jnp.bfloat16).reshape(-1, exp_here * hid),
+        expert_out.reshape(exp_here * hid, model_width),
         preferred_element_type=jnp.float32,
     )
-    hidden = (jax.nn.silu(gate_up[:, :, :, 0]) * gate_up[:, :, :, 1]).astype(jnp.bfloat16)
-    group_terms = jnp.einsum(
-        "sjch,jhd->sjcd", hidden, expert_out, preferred_element_type=jnp.float32
+    summed = lax.psum_scatter(
+        terms.astype(jnp.bfloat16), "tensor", scatter_dimension=1, tiled=True
     )
-    expert_rows_out = lax.psum_scatter(
-        group_terms.astype(jnp.bfloat16), "tensor", scatter_dimension=3, tiled=True
-    )
-    returned = lax.all_to_all(expert_rows_out, "seq", split_axis=0, concat_axis=0, tiled=True)
-    picked = returned.reshape(experts * capacity, slice_width)[places].reshape(
-        tok_rows, top_k, slice_width
-    )
-    mixture = jnp.sum(gate_weights[:, :, None] * picked.astype(jnp.float32), axis=1)
-    layer_out = (hidden_state + mixture).astype(jnp.bfloat16)
+    mixture = lax.psum_scatter(summed, "seq", scatter_dimension=0, tiled=True)
+    layer_out = (hidden_state + mixture.astype(jnp.float32)).astype(jnp.bfloat16)
     return (attended, layer_out)
 
 

time: 418 us -> 390 us (0.933)
  local copies, waits for them, and re-layouts: 62.1 us -> 37.1 us
  waiting for transfers between devices: 219 us -> 241 us
  blocking collectives: 61.6 us -> 49.6 us
  starting transfers between devices: 5.81 us -> 0.24 us
  other arithmetic: 21.2 us -> 16.7 us
    reduce_scatter x2 -> x3, waiting for transfers between devices: 78.2 us -> 138 us  [the longest x1 67.5 us: body(): mixture = lax.psum_scatter(summed, 'seq', scatter_dimension=0, tiled=True)]
    all_to_all x1 -> x0, blocking collectives: 42.5 us -> none  [body(): lax.all_to_all(outgoing.reshape(sources, exp_here, capacity, slice_width)...]
    all_to_all x1 -> x0, waiting for transfers between devices: 37 us -> none  [body(): lax.all_to_all(expert_rows_out, 'seq', split_axis=0, concat_axis=0, tiled...]
    all_gather x0 -> x1, blocking collectives: none -> 30.7 us  [body(): all_gates = lax.all_gather(gates, 'seq', axis=0, tiled=True)]
    scatter x1 -> x0, local copies, waits for them, and re-layouts: 7.33 us -> none  [body(): outgoing = jnp.zeros((experts * capacity, slice_width), jnp.bfloat16).at[...]
    all_to_all x1 -> x0, starting transfers between devices: 5.65 us -> none  [body(): lax.all_to_all(expert_rows_out, 'seq', split_axis=0, concat_axis=0, tiled...]
    gather x1 -> x0, local copies, waits for them, and re-layouts: 4.97 us -> none  [body(): returned.reshape(experts * capacity, slice_width)[places]]
    unnamed x26 -> x20, local copies, waits for them, and re-layouts: 11.3 us -> 12.7 us
  transfers between devices with their start and end apart: 5 -> 6, of which waited for: 5 -> 6; matrix products, arithmetic and copies ran while one was open for 2% -> 1% of each run, Pallas kernels for 0% -> 0%
where the time goes in v1:
time: 390 us; the launch traced here: 389 us
  waiting for transfers between devices  241 us (62%)
  blocking collectives  49.6 us (13%)
  local copies, waits for them, and re-layouts  37.1 us (10%)
  matrix products  23.2 us (6%)
  other arithmetic  16.7 us (4%)
  between operations  15 us (4%)
  loops' own time  5.98 us (2%)
    reduce_scatter x1, waiting for transfers between devices, body(): mixture = lax.psum_scatter(summed, 'seq', scatter_dimension=0, tiled=True)  67.5 us
    all_gather x1, waiting for transfers between devices, body(): cache_rows = lax.all_gather(own_cache, 'seq', axis=0, tiled=True)  58 us
    reduce_scatter x1, waiting for transfers between devices, body(): lax.psum_scatter(terms.astype(jnp.bfloat16), 'tensor', scatter_dimension=...  44.6 us
    all_gather x1, waiting for transfers between devices, body(): rows = lax.all_gather(normed, 'seq', axis=0, tiled=True)  41.4 us
    all_gather x1, blocking collectives, body(): all_gates = lax.all_gather(gates, 'seq', axis=0, tiled=True)  30.7 us
    reduce_scatter x1, waiting for transfers between devices, body(): lax.psum_scatter(projected.astype(jnp.bfloat16), 'tensor', scatter_dimens...  25.9 us
    unnamed x1, blocking collectives  13.1 us
    unnamed x20, local copies, waits for them, and re-layouts  12.7 us
  transfers between devices with their start and end apart: 6, of which 6 were waited for; matrix products, arithmetic and copies ran while one was open for 1% of the time, Pallas kernels for 0%

profile of v1, /device:TPU:0, one launch (start us, length us, event | category | flops | bytes accessed | tf_op | source)
XLA Modules:
  0.0 389.2 jit_solution(11495464832172759707)
XLA Ops:
  7.3 1.6 constant_dynamic-slice_fusion.2
  8.8 1.1 copy.65
  10.7 1.2 dynamic-slice
  11.9 0.8 dynamic-update-slice
  12.7 13.1 %all-reduce = s32[8]{0:T(128)S(1)} all-reduce(s32[8]{0:T(128)S(1)} %dynamic-update-slice), channel_id=1, replica_groups=mesh['seq'=8,'tensor'=4] {'seq'}, use_global_device_ids=true, to_apply=%add | all-reduce | flops 8 | bytes 64
  25.8 0.9 constant_dynamic-slice_fusion.1
  26.7 1.0 copy.50
  28.3 58.0 %all-gather.4.cloned.1.call-done = bf16[8192,256]{0,1:T(8,128)(2,1)} async-done(((bf16[1024,256]{0,1:T(8,128)(2,1)}), bf16[8192,256]{0,1:T(8,128)(2,1)}) %all-gather.4.cloned.1.call-update) | async-done | bytes 4194320 | tf_op jit(solution)/shard_map/all_gather | solution.py:66
  86.3 8.5 %copy.67 = bf16[32,8,8,1024]{3,2,1,0:T(8,128)(2,1)} copy(bf16[32,8,8,1024]{3,1,2,0:T(8,128)(2,1)} %bitcast.84) | data formatting | bytes 8388608
  94.8 6.6 %copy.51 = bf16[8,1024,2,128]{3,1,2,0:T(8,128)(2,1)} copy(bf16[8,1024,2,128]{1,0,3,2:T(8,128)(2,1)} %bitcast.83) | data formatting | bytes 8388608 | tf_op jit(solution)/shard_map/while | solution.py:83
  101.4 0.7 broadcast_in_dim.82
  102.1 34.2 %while.14 = (s32[]{:T(128)}, f32[128,4]{0,1:T(4,128)S(1)}, f32[128,4]{0,1:T(4,128)S(1)}, f32[128,4,128]{2,0,1:T(8,128)}, s32[8]{0:T(128)S(1)}, /*index=5*/s32[12...) while((s32[]{:T(128)}, f32[128,4]{0,1:T(4,128)S(1)}, ...), condition=%wide.region_7.8_spmd, body=%wide.region_1.7_spmd.sunk | while | flops 274334976 | bytes 10651687 | solution.py:83
  102.1 0.6 dynamic_slice.39
  102.7 1.3 fusion.38
  104.7 3.4 conditional.2
  104.7 1.1 dynamic-slice_bitcast_fusion
  105.9 0.4 bitcast_reduce_fusion
  106.8 0.6 convolution_add_fusion
  107.4 0.7 copy-done.3
  108.1 0.6 dynamic_slice.39
  108.7 1.3 fusion.38
  110.7 3.4 conditional.2
  110.7 1.1 dynamic-slice_bitcast_fusion
  111.8 0.4 bitcast_reduce_fusion
  112.7 0.6 convolution_add_fusion
  113.4 0.7 copy-done.3
  114.0 0.6 dynamic_slice.39
  114.6 1.3 fusion.38
  116.6 0.6 dynamic_slice.39
  117.2 1.3 fusion.38
  119.2 3.4 conditional.2
  119.2 1.1 dynamic-slice_bitcast_fusion
  120.4 0.4 bitcast_reduce_fusion
  121.3 0.6 convolution_add_fusion
  121.9 0.7 copy-done.3
  122.6 0.6 dynamic_slice.39
  123.2 1.3 fusion.38
  125.2 0.6 dynamic_slice.39
  125.8 1.3 fusion.38
  127.8 0.6 dynamic_slice.39
  128.4 1.3 fusion.38
  130.4 0.6 dynamic_slice.39
  131.0 1.3 fusion.38
  133.0 3.4 conditional.2
  133.0 1.1 dynamic-slice_bitcast_fusion
  134.2 0.4 bitcast_reduce_fusion
  135.1 0.6 convolution_add_fusion
  135.7 0.7 copy-done.3
  136.4 1.8 copy.55
  138.3 1.2 fusion.21
  139.5 2.9 convolution_convert_fusion
  142.5 0.8 dynamic_slice.28
  143.2 25.9 %reduce-scatter.4.cloned.1.call-done = bf16[128,512]{1,0:T(8,128)(2,1)} async-done(((bf16[128,2048]{1,0:T(8,128)(2,1)}), bf16[128,512]{1,0:T(8,128)(2,1)}) %reduce-scatter.4.cloned.1.call-update) | async-done | bytes 131088 | tf_op jit(solution)/shard_map/reduce_scatter | solution.py:99
  169.1 1.0 multiply_reduce_fusion
  170.1 5.8 %psum.7 = f32[128]{0:T(128)S(1)} all-reduce(f32[128]{0:T(128)S(1)} %multiply_reduce_fusion), channel_id=1, replica_groups=mesh['seq'=8,'tensor'=4] {'tensor'}, use_global_device_ids=true, to_apply=%region_12.13 | all-reduce | flops 128 | bytes 1024 | tf_op jit(solution)/shard_map/psum | solution.py:105
  175.9 1.7 multiply_convert_fusion
  177.6 41.4 %all-gather.6.cloned.1.call-done = bf16[1024,512]{1,0:T(8,128)(2,1)} async-done(((bf16[128,512]{1,0:T(8,128)(2,1)}), bf16[1024,512]{1,0:T(8,128)(2,1)}) %all-gather.6.cloned.1.call-update) | async-done | bytes 1048592 | tf_op jit(solution)/shard_map/all_gather | solution.py:118
  219.1 30.7 %all_gather.19 = f32[1024,16]{0,1:T(8,128)S(1)} all-gather(f32[128,16]{0,1:T(8,128)S(1)} %select_reduce_fusion), channel_id=1, replica_groups=mesh['seq'=8,'tensor'=4] {'seq'}, dimensions={0}, use_global_device_ids=true | all-gather | bytes 73728 | tf_op jit(solution)/shard_map/all_gather | solution.py:116
  249.8 4.0 %all-gather.8.cloned.1.call-done = bf16[1024,2048]{1,0:T(8,128)(2,1)} async-done(((bf16[1024,512]{1,0:T(8,128)(2,1)}), bf16[1024,2048]{1,0:T(8,128)(2,1)}) %all-gather.8.cloned.1.call-update) | async-done | bytes 4194320 | tf_op jit(solution)/shard_map/all_gather | solution.py:119
  253.8 9.4 %fusion.10 = f32[1024,2,2,352]{0,3,2,1:T(8,128)S(1)} fusion(bf16[2,2048,2,352]{1,3,2,0:T(8,128)(2,1)} %param.28, bf16[1024,2048]{1,0:T(8,128)(2,1)} %all-gather.8.cloned.1.call-done), kind=kOutput, calls=%fused_computation.20 | convolution fusion | flops 5905580032 | bytes 15728640 | tf_op jit(solution)/shard_map/rd,jdgh->rjgh/dot_general | solution.py:120
  263.2 5.2 %bitcast_convert_fusion = bf16[1024,2048]{1,0:T(8,128)(2,1)} fusion(bf16[2,352,2048]{2,1,0:T(8,128)(2,1)S(1)} %copy-done, f32[1024,2,2,352]{0,3,2,1:T(8,128)S(1)} %fusion.10, f32[1024,2]{0,1:T(2,128)S(1)} %constant_dynamic-slice_fusion), kind=kOutput, calls=%fused_computation.19 | convolution fusion | flops 2959933440 | bytes 12853248 | tf_op jit(solution)/shard_map/dot_general | solution.py:122
  268.5 44.6 %reduce-scatter.6.cloned.1.call-done = bf16[1024,512]{1,0:T(8,128)(2,1)} async-done(((bf16[1024,2048]{1,0:T(8,128)(2,1)}), bf16[1024,512]{1,0:T(8,128)(2,1)}) %reduce-scatter.6.cloned.1.call-update) | async-done | bytes 1048592 | tf_op jit(solution)/shard_map/reduce_scatter | solution.py:127
  313.2 67.5 %reduce-scatter.8.cloned.1.call-done = bf16[128,512]{1,0:T(8,128)(2,1)} async-done(((bf16[1024,512]{1,0:T(8,128)(2,1)}), bf16[128,512]{1,0:T(8,128)(2,1)}) %reduce-scatter.8.cloned.1.call-update) | async-done | bytes 131088 | tf_op jit(solution)/shard_map/reduce_scatter | solution.py:130
  380.6 1.7 add_convert_fusion
  (72 shorter events, 2.9 us)
Async XLA Ops:
  7.2 256.0 %copy-start = (bf16[2,352,2048]{2,1,0:T(8,128)(2,1)S(1)}, bf16[2,352,2048]{2,1,0:T(8,128)(2,1)}, u32[]{:S(2)}) copy-start(bf16[2,352,2048]{2,1,0:T(8,128)(2,1)} %param.29) | copy-start | bytes 8650756
  7.2 20.7 %copy-start.8 = (s32[1,4]{1,0:T(1,128)S(1)}, s32[1,4]{1,0:T(1,128)}, u32[]{:S(2)}) copy-start(s32[1,4]{1,0:T(1,128)} %param.20) | copy-start | bytes 52
  7.2 20.7 %copy-start.7 = (s32[1,128]{1,0:T(1,128)S(1)}, s32[1,128]{1,0:T(1,128)}, u32[]{:S(2)}) copy-start(s32[1,128]{1,0:T(1,128)} %param.19) | copy-start | bytes 1540
  7.2 79.1 %all-gather.4.cloned.1.call-start = ((), (), s32[]{:S(2)}) async-start(), calls=%async_computation.3 | async-start | bytes 4718592 | tf_op jit(solution)/shard_map/all_gather | solution.py:66
  10.0 159.1 %reduce-scatter.4.cloned.1.call-start = ((), (), s32[]{:S(2)}) async-start(), calls=%async_computation.4 | async-start | bytes 655360 | tf_op jit(solution)/shard_map/reduce_scatter | solution.py:99
  104.7 2.1 copy-start.2
  107.4 0.7 copy-start.3
  110.7 2.0 copy-start.2
  113.3 0.7 copy-start.3
  119.2 2.0 copy-start.2
  121.9 0.7 copy-start.3
  133.0 2.1 copy-start.2
  135.7 0.7 copy-start.3
  138.2 80.8 %copy-start.5 = (f32[128,6]{0,1:T(8,128)S(1)}, f32[128,6]{0,1:T(8,128)}, u32[]{:S(2)}) copy-start(f32[128,6]{0,1:T(8,128)} %param.27) | copy-start | bytes 9220
  138.2 80.8 %copy-start.6 = (s32[128,6]{0,1:T(8,128)S(1)}, s32[128,6]{0,1:T(8,128)}, u32[]{:S(2)}) copy-start(s32[128,6]{0,1:T(8,128)} %param.26) | copy-start | bytes 9220
  139.5 29.7 %copy-start.4 = (bf16[128,2048]{1,0:T(8,128)(2,1)S(1)}, bf16[128,2048]{1,0:T(8,128)(2,1)}, u32[]{:S(2)}) copy-start(bf16[128,2048]{1,0:T(8,128)(2,1)} %param.23) | copy-start | bytes 1572868
  142.4 76.6 %all-gather.6.cloned.1.call-start = ((), (), s32[]{:S(2)}) async-start(), calls=%async_computation.5 | async-start | bytes 1179648 | tf_op jit(solution)/shard_map/all_gather | solution.py:118
  177.6 76.2 %all-gather.8.cloned.1.call-start = ((), (), s32[]{:S(2)}) async-start(), calls=%async_computation.6 | async-start | bytes 5242880 | tf_op jit(solution)/shard_map/all_gather | solution.py:119
  219.0 94.1 %reduce-scatter.6.cloned.1.call-start = ((), (), s32[]{:S(2)}) async-start(), calls=%async_computation.7 | async-start | bytes 5242880 | tf_op jit(solution)/shard_map/reduce_scatter | solution.py:127
  268.5 112.2 %copy-start.1 = (bf16[128,512]{1,0:T(8,128)(2,1)S(1)}, bf16[128,512]{1,0:T(8,128)(2,1)}, u32[]{:S(2)}) copy-start(bf16[128,512]{1,0:T(8,128)(2,1)} %reduce-scatter.4.cloned.1.call-done) | copy-start | bytes 393220
  268.5 112.2 %reduce-scatter.8.cloned.1.call-start = ((), (), s32[]{:S(2)}) async-start(), calls=%async_computation.8 | async-start | bytes 1179648 | tf_op jit(solution)/shard_map/reduce_scatter | solution.py:130
Sparse Core Ops, SparseCore 0:
  10.2 76.0 all-gather.3
  142.5 26.5 reduce-scatter.3
  177.7 41.2 all-gather.5
  220.5 33.2 all-gather.7
  268.6 44.5 reduce-scatter.5
  316.4 64.1 reduce-scatter.7

commit v2 on v1

--- a/solution.py
+++ b/solution.py
@@ -1,6 +1,10 @@
+import functools
+
 import jax
 import jax.numpy as jnp
 from jax import lax
+from jax.experimental import pallas as pl
+from jax.experimental.pallas import tpu as pltpu
 from jax.sharding import PartitionSpec as P
 
 QH = 16
@@ -28,6 +32,337 @@
         running_sum * shrink + jnp.sum(weights, axis=2),
         weighted * shrink[:, :, None] + gathered,
     )
+
+
+MESH = pl.DeviceIdType.MESH
+
+
+def flipped(value, mask, bits):
+    out = 0
+    for b in range(bits):
+        one = lax.rem(lax.div(value, 1 << b), 2)
+        two = lax.rem(lax.div(mask, 1 << b), 2)
+        out = out + (one + two - 2 * one * two) * (1 << b)
+    return out
+
+
+def moe_kernel(
+    ns,
+    nt,
+    att,
+    wo,
+    res,
+    gain,
+    gates,
+    win_hbm,
+    wout_hbm,
+    attended,
+    layer,
+    win,
+    wout,
+    hid,
+    X,
+    S,
+    rc,
+    rx,
+    ry,
+    rz,
+    ps,
+    pr,
+    qs,
+    qr,
+    ls,
+    p_s,
+    p_r,
+    q_s,
+    q_r,
+    z_s,
+    z_r,
+    y_s,
+    y_r,
+    x_s,
+    x_r,
+    c_s,
+    c_r,
+    oc_s,
+    oc_r,
+    ox_s,
+    ox_r,
+    oy_s,
+    oy_r,
+    oz_s,
+    oz_r,
+):
+    rows, cols = res.shape
+    nq, nx = ns // 2, nt // 2
+    seq_bits, ten_bits = (ns - 1).bit_length(), (nt - 1).bit_length()
+    s, t = lax.axis_index("seq"), lax.axis_index("tensor")
+    i32 = jnp.int32
+
+    def across_s(mask):
+        return (flipped(s, i32(mask) if isinstance(mask, int) else mask, seq_bits), t)
+
+    def across_t(mask):
+        return (s, flipped(t, i32(mask), ten_bits))
+
+    load_in = pltpu.make_async_copy(win_hbm, win, ls.at[0])
+    load_out = pltpu.make_async_copy(wout_hbm, wout, ls.at[1])
+    load_in.start()
+    load_out.start()
+
+    barrier = pltpu.get_barrier_semaphore()
+    for k in range(1, nt):
+        pl.semaphore_signal(barrier, inc=1, device_id=across_t(k), device_id_type=MESH)
+    pl.semaphore_signal(barrier, inc=1, device_id=across_s(1), device_id_type=MESH)
+    for q in range(1, nq):
+        pl.semaphore_signal(barrier, inc=1, device_id=across_s(2 * q), device_id_type=MESH)
+    pl.semaphore_wait(barrier, nt - 1 + nq)
+
+    def move(src, dst, send, recv, dev):
+        return pltpu.make_async_remote_copy(
+            src_ref=src,
+            dst_ref=dst,
+            send_sem=send,
+            recv_sem=recv,
+            device_id=dev,
+            device_id_type=MESH,
+        )
+
+    def both(q):
+        return pl.ds(pl.multiple_of(q * 2 * rows, 2 * rows), 2 * rows)
+
+    def half(q, pos):
+        return pl.ds(pl.multiple_of((q * 2 + pos) * rows, rows), rows)
+
+    def proj(k):
+        return move(ps.at[k], pr.at[k], p_s.at[k], p_r.at[k], across_t(k))
+
+    def sq(k):
+        return move(qs, qr.at[k], q_s.at[k], q_r.at[k], across_t(k))
+
+    def z_go(q):
+        return move(
+            X.at[0, half(0, 0)], X.at[0, half(q, 0)], z_s.at[q], z_r.at[q], across_s(2 * q)
+        )
+
+    def y_go(q):
+        return move(
+            X.at[0, half(q, 0)], X.at[0, half(q, 1)], y_s.at[q], y_r.at[q], across_s(1)
+        )
+
+    def x_go(q, a):
+        return move(
+            X.at[0, both(q)], X.at[2 * a, both(q)], x_s.at[q, a], x_r.at[q, a], across_t(2 * a)
+        )
+
+    def c_go(q, a):
+        return move(
+            X.at[2 * a, both(q)], X.at[2 * a + 1, both(q)], c_s.at[q, a], c_r.at[q, a], across_t(1)
+        )
+
+    def c_back(q, a):
+        return move(
+            S.at[2 * a + 1, both(q)], rc.at[a, both(q)], oc_s.at[q, a], oc_r.at[q, a], across_t(1)
+        )
+
+    def x_back(q, a):
+        return move(
+            S.at[2 * a, both(q)], rx.at[a - 1, both(q)], ox_s.at[q, a], ox_r.at[q, a], across_t(2 * a)
+        )
+
+    def y_back(q):
+        return move(S.at[0, half(q, 1)], ry.at[q], oy_s.at[q], oy_r.at[q], across_s(1))
+
+    def z_back(q):
+        return move(S.at[0, half(q, 0)], rz.at[q], oz_s.at[q], oz_r.at[q], across_s(2 * q))
+
+    def wide(k):
+        return pl.ds(pl.multiple_of(flipped(t, i32(k), ten_bits) * cols, cols), cols)
+
+    a_rows = att[...]
+    for k in [*range(2, nt), 1]:
+        ps[k] = jnp.dot(a_rows, wo[:, wide(k)], preferred_element_type=jnp.float32).astype(
+            jnp.bfloat16
+        )
+        proj(k).start()
+    total = res[...].astype(jnp.float32) + jnp.dot(
+        a_rows, wo[:, wide(0)], preferred_element_type=jnp.float32
+    )
+    for k in range(1, nt):
+        proj(k).wait_recv()
+        total = total + pr[k].astype(jnp.float32)
+    attended[...] = total.astype(jnp.bfloat16)
+    hid[...] = total
+    own_sq = jnp.sum(total * total, axis=1, keepdims=True)
+    qs[...] = jnp.broadcast_to(own_sq, (rows, rows)).T[:8]
+    for k in range(1, nt):
+        sq(k).start()
+    all_sq = qs[...]
+    for k in range(1, nt):
+        sq(k).wait_recv()
+        all_sq = all_sq + qr[k]
+    scale = lax.rsqrt(all_sq / (cols * nt) + 1e-06)
+    scale = jnp.broadcast_to(scale[:1], (rows, rows)).T[:, :1]
+    X[0, 0:rows, :] = (total * scale * gain[...]).astype(jnp.bfloat16)
+
+    y_go(0).start()
+    for q in range(1, nq):
+        z_go(q).start()
+
+    def spread_y(q, _):
+        z_go(q).wait_recv()
+        y_go(q).start()
+        return 0
+
+    lax.fori_loop(1, nq, spread_y, 0)
+
+    def spread_x(q, _):
+        y_go(q).wait_recv()
+        for a in range(1, nx):
+            x_go(q, a).start()
+        c_go(q, 0).start()
+        return 0
+
+    lax.fori_loop(0, nq, spread_x, 0)
+    load_in.wait()
+    load_out.wait()
+
+    def experts(q):
+        for a in range(1, nx):
+            x_go(q, a).wait_recv()
+            c_go(q, a).start()
+        up, gate = None, None
+        for k in [*range(0, nt, 2), *range(1, nt, 2)]:
+            if k % 2:
+                c_go(q, k // 2).wait_recv()
+            x = X[k, both(q), :]
+            part = wide(k)
+            g = jnp.dot(x, win[0, part, :], preferred_element_type=jnp.float32)
+            u = jnp.dot(x, win[1, part, :], preferred_element_type=jnp.float32)
+            gate = g if gate is None else gate + g
+            up = u if up is None else up + u
+        width = gate.shape[1]
+        own = gates[both(q), :]
+        each = width // own.shape[1]
+        column = lax.broadcasted_iota(jnp.int32, gate.shape, 1)
+        weight = own[:, 0:1]
+        for j in range(1, own.shape[1]):
+            weight = jnp.where(column >= j * each, own[:, j : j + 1], weight)
+        hidden = (gate / (1.0 + jnp.exp(-gate)) * up * weight).astype(jnp.bfloat16)
+        for k in [*range(1, nt, 2), *range(0, nt, 2)]:
+            S[k, both(q), :] = jnp.dot(
+                hidden, wout[:, wide(k)], preferred_element_type=jnp.float32
+            ).astype(jnp.bfloat16)
+            if k % 2:
+                c_back(q, k // 2).start()
+
+    def step(i, _):
+        @pl.when(i < nq)
+        def _():
+            experts(i)
+
+        @pl.when((i >= 1) & (i < nq + 1))
+        def _():
+            q = i - 1
+            for a in [*range(1, nx), 0]:
+                c_back(q, a).wait_recv()
+                S[2 * a, both(q), :] = (
+                    S[2 * a, both(q), :].astype(jnp.float32)
+                    + rc[a, both(q), :].astype(jnp.float32)
+                ).astype(jnp.bfloat16)
+                if a:
+                    x_back(q, a).start()
+
+        @pl.when((i >= 2) & (i < nq + 2))
+        def _():
+            q = i - 2
+            acc = S[0, both(q), :].astype(jnp.float32)
+            for a in range(1, nx):
+                x_back(q, a).wait_recv()
+                acc = acc + rx[a - 1, both(q), :].astype(jnp.float32)
+            S[0, both(q), :] = acc.astype(jnp.bfloat16)
+            y_back(q).start()
+
+        @pl.when(i >= 3)
+        def _():
+            q = i - 3
+            y_back(q).wait_recv()
+            S[0, half(q, 0), :] = (
+                S[0, half(q, 0), :].astype(jnp.float32) + ry[q].astype(jnp.float32)
+            ).astype(jnp.bfloat16)
+
+            @pl.when(q > 0)
+            def _():
+                z_back(q).start()
+
+        return 0
+
+    lax.fori_loop(0, nq + 3, step, 0)
+    out = hid[...] + S[0, half(0, 0), :].astype(jnp.float32)
+    for q in range(1, nq):
+        z_back(q).wait_recv()
+        out = out + rz[q].astype(jnp.float32)
+    layer[...] = out.astype(jnp.bfloat16)
+
+    for k in range(1, nt):
+        proj(k).wait_send()
+        sq(k).wait_send()
+
+    def drain(q, _):
+        @pl.when(q > 0)
+        def _():
+            z_go(q).wait_send()
+            z_back(q).wait_send()
+
+        y_go(q).wait_send()
+        y_back(q).wait_send()
+        for a in range(nx):
+            if a:
+                x_go(q, a).wait_send()
+                x_back(q, a).wait_send()
+            c_go(q, a).wait_send()
+            c_back(q, a).wait_send()
+        return 0
+
+    lax.fori_loop(0, nq, drain, 0)
+
+
+def moe(ns, nt, att, wo, res, gain, gates, win, wout):
+    rows, cols = res.shape
+    nq, nx = ns // 2, nt // 2
+    bf = jnp.bfloat16
+    dma = pltpu.SemaphoreType.DMA
+    vmem = pl.BlockSpec(memory_space=pltpu.VMEM)
+    anywhere = pl.BlockSpec(memory_space=pl.ANY)
+    everyone = ns * rows
+    scratch = [
+        pltpu.VMEM(win.shape, bf),
+        pltpu.VMEM(wout.shape, bf),
+        pltpu.VMEM((rows, cols), jnp.float32),
+        pltpu.VMEM((nt, everyone, cols), bf),
+        pltpu.VMEM((nt, everyone, cols), bf),
+        pltpu.VMEM((nx, everyone, cols), bf),
+        pltpu.VMEM((nx - 1, everyone, cols), bf),
+        pltpu.VMEM((nq, rows, cols), bf),
+        pltpu.VMEM((nq, rows, cols), bf),
+        pltpu.VMEM((nt, rows, cols), bf),
+        pltpu.VMEM((nt, rows, cols), bf),
+        pltpu.VMEM((8, rows), jnp.float32),
+        pltpu.VMEM((nt, 8, rows), jnp.float32),
+        dma((2,)),
+    ]
+    for shape in [(nt,), (nt,), (nq,), (nq,), (nq, nx), (nq, nx), (nq, nx), (nq, nx), (nq,), (nq,)]:
+        scratch += [dma(shape), dma(shape)]
+    return pl.pallas_call(
+        functools.partial(moe_kernel, ns, nt),
+        out_shape=[jax.ShapeDtypeStruct((rows, cols), bf)] * 2,
+        in_specs=[vmem] * 5 + [anywhere] * 2,
+        out_specs=[vmem] * 2,
+        scratch_shapes=scratch,
+        compiler_params=pltpu.CompilerParams(
+            collective_id=1, has_side_effects=True, vmem_limit_bytes=62 * 2**20
+        ),
+    )(att, wo, res, gain, gates, win, wout)
 
 
 def body(
@@ -64,7 +399,20 @@
     shard_len = prefix_kv.shape[0]
     own_cache = lax.dynamic_slice_in_dim(prefix_kv, kv_head, 1, 1).reshape(shard_len, 2 * head_size)
     cache_rows = lax.all_gather(own_cache, "seq", axis=0, tiled=True)
-    owners = lax.all_gather(shard_prefix, "seq", axis=0, tiled=True)
+    exp_here = expert_in.shape[0]
+    members = lax.axis_size("seq")
+    experts = exp_here * members
+    named = expert_ids[:, :, None] == jnp.arange(experts, dtype=jnp.int32)[None, None, :]
+    gates = jnp.sum(jnp.where(named, gate_weights[:, :, None], 0.0), axis=1)
+    owner_rows = jnp.broadcast_to(shard_prefix.astype(jnp.float32)[:, None], (8, experts))
+    small = lax.all_gather(jnp.concatenate([gates, owner_rows], axis=0), "seq", axis=0)
+    owners = small[:, tok_rows, 0].astype(jnp.int32)
+    me = lax.axis_index("seq")
+    own_gates = lax.dynamic_slice_in_dim(small[:, :tok_rows], me * exp_here, exp_here, 2)
+    index = jnp.arange(members, dtype=jnp.int32)
+    chosen = (index ^ me)[:, None] == index[None, :]
+    own_gates = jnp.sum(jnp.where(chosen[:, :, None, None], own_gates[None], 0.0), axis=1)
+    own_gates = own_gates.reshape(members * tok_rows, exp_here)
     shard_count = owners.shape[0]
     shards = cache_rows.reshape(shard_count, -1, 2, head_size)
 
@@ -92,44 +440,23 @@
         .reshape(tok_rows, heads_here * head_size)
         .astype(jnp.bfloat16)
     )
-    projected = jnp.dot(attention, out_weight, preferred_element_type=jnp.float32)
-    model_width = residual.shape[1]
-    slice_width = model_width // lax.axis_size("tensor")
+    slice_width = query.shape[1]
     first_col = lax.axis_index("tensor") * slice_width
-    shared = lax.psum_scatter(
-        projected.astype(jnp.bfloat16), "tensor", scatter_dimension=1, tiled=True
-    )
-    hidden_state = lax.dynamic_slice_in_dim(residual, first_col, slice_width, 1).astype(
-        jnp.float32
-    ) + shared.astype(jnp.float32)
-    squares = lax.psum(jnp.sum(hidden_state * hidden_state, axis=1), "tensor")
-    gain_cols = lax.dynamic_slice_in_dim(norm_gain, first_col, slice_width, 0)
-    normed = (
-        hidden_state * lax.rsqrt(squares / model_width + 1e-06)[:, None] * gain_cols[None, :]
-    ).astype(jnp.bfloat16)
-    attended = hidden_state.astype(jnp.bfloat16)
-    exp_here = expert_in.shape[0]
-    hid = expert_in.shape[3]
-    experts = exp_here * lax.axis_size("seq")
-    named = expert_ids[:, :, None] == jnp.arange(experts, dtype=jnp.int32)[None, None, :]
-    gates = jnp.sum(jnp.where(named, gate_weights[:, :, None], 0.0), axis=1)
-    all_gates = lax.all_gather(gates, "seq", axis=0, tiled=True)
-    own_gates = lax.dynamic_slice_in_dim(all_gates, lax.axis_index("seq") * exp_here, exp_here, 1)
-    rows = lax.all_gather(normed, "seq", axis=0, tiled=True)
-    rows = lax.all_gather(rows, "tensor", axis=1, tiled=True)
-    gate_up = jnp.einsum("rd,jdgh->rjgh", rows, expert_in, preferred_element_type=jnp.float32)
-    hidden = jax.nn.silu(gate_up[:, :, 0]) * gate_up[:, :, 1] * own_gates[:, :, None]
-    terms = jnp.dot(
-        hidden.astype(jnp.bfloat16).reshape(-1, exp_here * hid),
-        expert_out.reshape(exp_here * hid, model_width),
-        preferred_element_type=jnp.float32,
-    )
-    summed = lax.psum_scatter(
-        terms.astype(jnp.bfloat16), "tensor", scatter_dimension=1, tiled=True
-    )
-    mixture = lax.psum_scatter(summed, "seq", scatter_dimension=0, tiled=True)
-    layer_out = (hidden_state + mixture.astype(jnp.float32)).astype(jnp.bfloat16)
-    return (attended, layer_out)
+    width = exp_here * expert_in.shape[3]
+    win = jnp.transpose(expert_in, (2, 1, 0, 3)).reshape(2, expert_in.shape[1], width)
+    return tuple(
+        moe(
+            lax.axis_size("seq"),
+            lax.axis_size("tensor"),
+            attention,
+            out_weight,
+            lax.dynamic_slice_in_dim(residual, first_col, slice_width, 1),
+            lax.dynamic_slice_in_dim(norm_gain, first_col, slice_width, 0)[None, :],
+            own_gates,
+            win,
+            expert_out.reshape(width, expert_out.shape[2]),
+        )
+    )
 
 
 def solution(mesh):

time: 390 us -> 239 us (0.61)
  waiting for transfers between devices: 241 us -> 23.6 us
  Pallas kernels: 0 us -> 84 us
  local copies, waits for them, and re-layouts: 37.1 us -> 54.8 us
  blocking collectives: 49.6 us -> 32.8 us
  matrix products: 23.2 us -> 8.89 us
    reduce_scatter x3 -> x0, waiting for transfers between devices: 138 us -> none  [the longest x1 67.5 us: body(): mixture = lax.psum_scatter(summed, 'seq', scatter_dimension=0, tiled=True)]
    pallas_call x0 -> x1, Pallas kernels: none -> 84 us  [moe(): pl.pallas_call(functools.partial(moe_kernel, ns, nt), out_shape=[jax.Shap...]
    all_gather x2 -> x0, waiting for transfers between devices: 45.3 us -> none  [the longest x1 41.4 us: body(): rows = lax.all_gather(normed, 'seq', axis=0, tiled=True)]
    all_gather x1, waiting for transfers between devices: 58 us -> 23.5 us  [body(): cache_rows = lax.all_gather(own_cache, 'seq', axis=0, tiled=True)]
    dot_general x3 -> x0, matrix products: 17.6 us -> none  [the longest x1 9.45 us: body(): jnp.einsum('rd,jdgh->rjgh', rows, expert_in, preferred_element_type=jnp.f...]
    unnamed x1 -> x0, blocking collectives: 13.1 us -> none
    reshape x0 -> x1, local copies, waits for them, and re-layouts: none -> 8.56 us  [body(): jnp.transpose(expert_in, (2, 1, 0, 3)).reshape(2, expert_in.shape[1], width)]
    unnamed x20 -> x19, local copies, waits for them, and re-layouts: 12.7 us -> 19.5 us
  transfers between devices with their start and end apart: 6 -> 1, of which waited for: 6 -> 1; matrix products, arithmetic and copies ran while one was open for 1% -> 8% of each run, Pallas kernels for 0% -> 0%
where the time goes in v2:
time: 239 us; the launch traced here: 240 us
  Pallas kernels  84 us (35%)
  local copies, waits for them, and re-layouts  54.8 us (23%)
  blocking collectives  32.8 us (14%)
  waiting for transfers between devices  23.6 us (10%)
  between operations  14.9 us (6%)
  other arithmetic  14.7 us (6%)
  matrix products  8.89 us (4%)
  loops' own time  6.04 us (3%)
    pallas_call x1, Pallas kernels, moe(): pl.pallas_call(functools.partial(moe_kernel, ns, nt), out_shape=[jax.Shap...  84 us
    all_gather x1, blocking collectives, body(): lax.all_gather(jnp.concatenate([gates, owner_rows], axis=0), 'seq', axis=0)  32.8 us
    all_gather x1, waiting for transfers between devices, body(): cache_rows = lax.all_gather(own_cache, 'seq', axis=0, tiled=True)  23.5 us
    unnamed x19, local copies, waits for them, and re-layouts  19.5 us
    reduce_or x8, other arithmetic, one_shard(): jnp.any(matching)  10.4 us
    squeeze x8, local copies, waits for them, and re-layouts, body(): final_state, unused = lax.scan(one_shard, blank_state, (shards, owners))  8.67 us
    reshape x1, local copies, waits for them, and re-layouts, body(): jnp.transpose(expert_in, (2, 1, 0, 3)).reshape(2, expert_in.shape[1], width)  8.56 us
    while x3, local copies, waits for them, and re-layouts, body(): final_state, unused = lax.scan(one_shard, blank_state, (shards, owners))  6.9 us
  transfers between devices with their start and end apart: 1, of which 1 were waited for; matrix products, arithmetic and copies ran while one was open for 8% of the time, Pallas kernels for 0%

profile of v2, /device:TPU:0, one launch (start us, length us, event | category | flops | bytes accessed | tf_op | source)
XLA Modules:
  0.0 239.7 jit_solution(17280289148675325637)
XLA Ops:
  7.3 1.5 constant_dynamic-slice_fusion.3
  8.7 1.1 copy.93
  10.5 0.9 constant_dynamic-slice_fusion.2
  11.5 32.8 %all-gather.1 = f32[8,136,16]{1,2,0:T(8,128)S(1)} all-gather(f32[1,136,16]{1,2,0:T(8,128)S(1)} %pad_bitcast_fusion), channel_id=2, replica_groups=mesh['seq'=8,'tensor'=4] {'seq'}, dimensions={0}, use_global_device_ids=true | all-gather | bytes 78336 | tf_op jit(solution)/shard_map/all_gather | solution.py:408
  44.8 1.0 copy.84
  45.8 6.6 %copy.85 = bf16[2,2048,2,352]{1,3,0,2:T(8,128)(2,1)} copy(bf16[2,2048,2,352]{1,3,2,0:T(8,128)(2,1)} %param.28) | data formatting | bytes 11534336 | tf_op args[11]
  52.4 8.6 %copy.86.win_hbm = bf16[2,2048,704]{2,1,0:T(8,128)(2,1)} copy(bf16[2,2048,704]{1,2,0:T(8,128)(2,1)} %bitcast.64) | data formatting | bytes 11534336 | tf_op jit(solution)/shard_map/reshape | solution.py:446
  61.0 1.4 dynamic_slice.28
  62.6 0.7 constant_dynamic-slice_fusion.1.res
  63.6 23.5 %all-gather.4.cloned.1.call-done = bf16[8192,256]{0,1:T(8,128)(2,1)} async-done(((bf16[1024,256]{0,1:T(8,128)(2,1)}), bf16[8192,256]{0,1:T(8,128)(2,1)}) %all-gather.4.cloned.1.call-update) | async-done | bytes 4194320 | tf_op jit(solution)/shard_map/all_gather | solution.py:401
  87.1 8.5 %copy.94 = bf16[32,8,8,1024]{3,2,1,0:T(8,128)(2,1)} copy(bf16[32,8,8,1024]{3,1,2,0:T(8,128)(2,1)} %bitcast.66) | data formatting | bytes 8388608
  95.7 6.6 %copy.75 = bf16[8,1024,2,128]{3,1,2,0:T(8,128)(2,1)} copy(bf16[8,1024,2,128]{1,0,3,2:T(8,128)(2,1)} %bitcast.65) | data formatting | bytes 8388608 | tf_op jit(solution)/shard_map/while | solution.py:431
  102.3 42.1 %while.14 = (s32[]{:T(128)}, f32[128,4]{0,1:T(4,128)S(1)}, f32[128,4]{0,1:T(4,128)S(1)}, f32[128,4,128]{2,0,1:T(8,128)S(1)}, s32[8]{0:T(128)S(1)}, /*index=5*/s3...) while((s32[]{:T(128)}, f32[128,4]{0,1:T(4,128)S(1)}, ...), condition=%wide.region_8.9_spmd, body=%wide.region_2.0_spmd.sunk | while | flops 274334976 | bytes 8554479 | solution.py:431
  102.4 0.6 dynamic_slice.36
  103.0 1.3 fusion.25
  105.0 2.6 %conditional.2 = ((f32[128,4]{0,1:T(4,128)S(1)}, f32[128,4]{0,1:T(4,128)S(1)}, f32[128,4,128]{2,0,1:T(8,128)S(1)})) conditional(s32[]{:T(128)} %convert_element_type.39, (f32[128,4]{0,1:T(4,128)S(1)}, f32[128,4]{0,1:T(4,128)S(1)}, f32[128,4,128]{2,0,1:T(8,128)S(1)}) %tuple.43, (pred[128]{0:T(512)(128)(4,1)S(1)}, bf16[8,1024,2,128]{3,1,2,0:T(8,128)(2,1)}, ...), branch_computations={%region_4.4_spmd, %region_5.7_spmd} | conditional | flops 274334720 | bytes 8553636 | solution.py:429
  105.0 1.1 dynamic-slice_bitcast_fusion
  107.0 0.6 convolution_add_fusion
  107.6 0.6 dynamic_slice.36
  108.2 1.3 fusion.25
  110.2 2.6 %conditional.2 = ((f32[128,4]{0,1:T(4,128)S(1)}, f32[128,4]{0,1:T(4,128)S(1)}, f32[128,4,128]{2,0,1:T(8,128)S(1)})) conditional(s32[]{:T(128)} %convert_element_type.39, (f32[128,4]{0,1:T(4,128)S(1)}, f32[128,4]{0,1:T(4,128)S(1)}, f32[128,4,128]{2,0,1:T(8,128)S(1)}) %tuple.43, (pred[128]{0:T(512)(128)(4,1)S(1)}, bf16[8,1024,2,128]{3,1,2,0:T(8,128)(2,1)}, ...), branch_computations={%region_4.4_spmd, %region_5.7_spmd} | conditional | flops 274334720 | bytes 8553636 | solution.py:429
  110.2 1.1 dynamic-slice_bitcast_fusion
  111.3 0.4 bitcast_reduce_fusion
  112.2 0.6 convolution_add_fusion
  112.9 0.6 dynamic_slice.36
  113.5 1.3 fusion.25
  115.5 2.6 %conditional.2 = ((f32[128,4]{0,1:T(4,128)S(1)}, f32[128,4]{0,1:T(4,128)S(1)}, f32[128,4,128]{2,0,1:T(8,128)S(1)})) conditional(s32[]{:T(128)} %convert_element_type.39, (f32[128,4]{0,1:T(4,128)S(1)}, f32[128,4]{0,1:T(4,128)S(1)}, f32[128,4,128]{2,0,1:T(8,128)S(1)}) %tuple.43, (pred[128]{0:T(512)(128)(4,1)S(1)}, bf16[8,1024,2,128]{3,1,2,0:T(8,128)(2,1)}, ...), branch_computations={%region_4.4_spmd, %region_5.7_spmd} | conditional | flops 274334720 | bytes 8553636 | solution.py:429
  115.5 1.1 dynamic-slice_bitcast_fusion
  116.6 0.4 bitcast_reduce_fusion
  117.5 0.6 convolution_add_fusion
  118.2 0.6 dynamic_slice.36
  118.8 1.3 fusion.25
  120.8 2.6 %conditional.2 = ((f32[128,4]{0,1:T(4,128)S(1)}, f32[128,4]{0,1:T(4,128)S(1)}, f32[128,4,128]{2,0,1:T(8,128)S(1)})) conditional(s32[]{:T(128)} %convert_element_type.39, (f32[128,4]{0,1:T(4,128)S(1)}, f32[128,4]{0,1:T(4,128)S(1)}, f32[128,4,128]{2,0,1:T(8,128)S(1)}) %tuple.43, (pred[128]{0:T(512)(128)(4,1)S(1)}, bf16[8,1024,2,128]{3,1,2,0:T(8,128)(2,1)}, ...), branch_computations={%region_4.4_spmd, %region_5.7_spmd} | conditional | flops 274334720 | bytes 8553636 | solution.py:429
  120.8 1.1 dynamic-slice_bitcast_fusion
  121.9 0.4 bitcast_reduce_fusion
  122.8 0.6 convolution_add_fusion
  123.4 0.6 dynamic_slice.36
  124.0 1.3 fusion.25
  126.0 2.6 %conditional.2 = ((f32[128,4]{0,1:T(4,128)S(1)}, f32[128,4]{0,1:T(4,128)S(1)}, f32[128,4,128]{2,0,1:T(8,128)S(1)})) conditional(s32[]{:T(128)} %convert_element_type.39, (f32[128,4]{0,1:T(4,128)S(1)}, f32[128,4]{0,1:T(4,128)S(1)}, f32[128,4,128]{2,0,1:T(8,128)S(1)}) %tuple.43, (pred[128]{0:T(512)(128)(4,1)S(1)}, bf16[8,1024,2,128]{3,1,2,0:T(8,128)(2,1)}, ...), branch_computations={%region_4.4_spmd, %region_5.7_spmd} | conditional | flops 274334720 | bytes 8553636 | solution.py:429
  126.0 1.1 dynamic-slice_bitcast_fusion
  127.1 0.4 bitcast_reduce_fusion
  128.0 0.6 convolution_add_fusion
  128.7 0.6 dynamic_slice.36
  129.3 1.3 fusion.25
  131.3 2.6 %conditional.2 = ((f32[128,4]{0,1:T(4,128)S(1)}, f32[128,4]{0,1:T(4,128)S(1)}, f32[128,4,128]{2,0,1:T(8,128)S(1)})) conditional(s32[]{:T(128)} %convert_element_type.39, (f32[128,4]{0,1:T(4,128)S(1)}, f32[128,4]{0,1:T(4,128)S(1)}, f32[128,4,128]{2,0,1:T(8,128)S(1)}) %tuple.43, (pred[128]{0:T(512)(128)(4,1)S(1)}, bf16[8,1024,2,128]{3,1,2,0:T(8,128)(2,1)}, ...), branch_computations={%region_4.4_spmd, %region_5.7_spmd} | conditional | flops 274334720 | bytes 8553636 | solution.py:429
  131.3 1.1 dynamic-slice_bitcast_fusion
  132.4 0.4 bitcast_reduce_fusion
  133.3 0.6 convolution_add_fusion
  134.0 0.6 dynamic_slice.36
  134.6 1.3 fusion.25
  136.6 2.6 %conditional.2 = ((f32[128,4]{0,1:T(4,128)S(1)}, f32[128,4]{0,1:T(4,128)S(1)}, f32[128,4,128]{2,0,1:T(8,128)S(1)})) conditional(s32[]{:T(128)} %convert_element_type.39, (f32[128,4]{0,1:T(4,128)S(1)}, f32[128,4]{0,1:T(4,128)S(1)}, f32[128,4,128]{2,0,1:T(8,128)S(1)}) %tuple.43, (pred[128]{0:T(512)(128)(4,1)S(1)}, bf16[8,1024,2,128]{3,1,2,0:T(8,128)(2,1)}, ...), branch_computations={%region_4.4_spmd, %region_5.7_spmd} | conditional | flops 274334720 | bytes 8553636 | solution.py:429
  136.6 1.1 dynamic-slice_bitcast_fusion
  137.7 0.4 bitcast_reduce_fusion
  138.6 0.6 convolution_add_fusion
  139.2 0.6 dynamic_slice.36
  139.8 1.3 fusion.25
  141.8 2.6 %conditional.2 = ((f32[128,4]{0,1:T(4,128)S(1)}, f32[128,4]{0,1:T(4,128)S(1)}, f32[128,4,128]{2,0,1:T(8,128)S(1)})) conditional(s32[]{:T(128)} %convert_element_type.39, (f32[128,4]{0,1:T(4,128)S(1)}, f32[128,4]{0,1:T(4,128)S(1)}, f32[128,4,128]{2,0,1:T(8,128)S(1)}) %tuple.43, (pred[128]{0:T(512)(128)(4,1)S(1)}, bf16[8,1024,2,128]{3,1,2,0:T(8,128)(2,1)}, ...), branch_computations={%region_4.4_spmd, %region_5.7_spmd} | conditional | flops 274334720 | bytes 8553636 | solution.py:429
  141.8 1.1 dynamic-slice_bitcast_fusion
  142.9 0.4 bitcast_reduce_fusion
  143.8 0.6 convolution_add_fusion
  145.0 0.8 copy.92.att
  145.7 84.0 %shard_map.140 = (bf16[128,512]{1,0:T(8,128)(2,1)}, bf16[128,512]{1,0:T(8,128)(2,1)}) custom-call(bf16[128,512]{1,0:T(8,128)(2,1)} %copy.92.att, bf16[512,2048]{1,0:T(8,128)(2,1)} %wo.1, bf16[128,512]{1,0:T(8,128)(2,1)} %constant_dynamic-slice_fusion.1.res, f32[1,512]{1,0:T(1,128)} %bitcast.75, f32[1024,2]{1,0:T(8,128)} %bitcast.68, ...), custom_call_target="tpu_custom_call" | custom-call | tf_op jit(solution)/shard_map/pallas_call | solution.py:356
  229.8 1.6 copy.119
  231.3 1.6 copy.120
  (70 shorter events, 5.7 us)
Async XLA Ops:
  7.2 55.5 %copy-start = (bf16[128,2048]{1,0:T(8,128)(2,1)S(1)}, bf16[128,2048]{1,0:T(8,128)(2,1)}, u32[]{:S(2)}) copy-start(bf16[128,2048]{1,0:T(8,128)(2,1)} %param.23) | copy-start | bytes 1572868
  7.2 4.3 %copy-start.2 = (f32[128,6]{0,1:T(8,128)S(1)}, f32[128,6]{0,1:T(8,128)}, u32[]{:S(2)}) copy-start(f32[128,6]{0,1:T(8,128)} %param.27) | copy-start | bytes 9220
  7.2 4.3 %copy-start.3 = (s32[128,6]{0,1:T(8,128)S(1)}, s32[128,6]{0,1:T(8,128)}, u32[]{:S(2)}) copy-start(s32[128,6]{0,1:T(8,128)} %param.26) | copy-start | bytes 9220
  7.2 37.1 %copy-start.1 = (bf16[128,512]{1,0:T(8,128)(2,1)S(1)}, bf16[128,512]{1,0:T(8,128)(2,1)}, u32[]{:S(2)}) copy-start(bf16[128,512]{1,0:T(8,128)(2,1)} %param.17) | copy-start | bytes 393220
  7.2 79.9 %all-gather.4.cloned.1.call-start = ((), (), s32[]{:S(2)}) async-start(), calls=%async_computation | async-start | bytes 4718592 | tf_op jit(solution)/shard_map/all_gather | solution.py:401
  52.4 10.2 %copy-start.4 = (s32[1,128]{1,0:T(1,128)S(1)}, s32[1,128]{1,0:T(1,128)}, u32[]{:S(2)}) copy-start(s32[1,128]{1,0:T(1,128)} %param.19) | copy-start | bytes 1540
  52.4 10.2 %copy-start.5 = (s32[1,4]{1,0:T(1,128)S(1)}, s32[1,4]{1,0:T(1,128)}, u32[]{:S(2)}) copy-start(s32[1,4]{1,0:T(1,128)} %param.20) | copy-start | bytes 52
Sparse Core Ops, SparseCore 0:
  10.2 76.8 all-gather.3

commit v3 on v2

--- a/solution.py
+++ b/solution.py
@@ -9,29 +9,6 @@
 
 QH = 16
 KVH = 4
-
-
-NEG_FLOOR = -1e30
-
-
-def fold_block(carried, queries, key_rows, values, allowed, score_scale):
-    running_max, running_sum, weighted = carried
-    scores = (
-        jnp.einsum("rhd,kd->rhk", queries, key_rows, preferred_element_type=jnp.float32)
-        * score_scale
-    )
-    scores = jnp.where(allowed[:, None, :], scores, -jnp.inf)
-    new_max = jnp.maximum(running_max, jnp.max(scores, axis=2))
-    weights = jnp.exp(scores - new_max[:, :, None])
-    shrink = jnp.exp(running_max - new_max)
-    gathered = jnp.einsum(
-        "rhk,kd->rhd", weights.astype(jnp.bfloat16), values, preferred_element_type=jnp.float32
-    )
-    return (
-        new_max,
-        running_sum * shrink + jnp.sum(weights, axis=2),
-        weighted * shrink[:, :, None] + gathered,
-    )
 
 
 MESH = pl.DeviceIdType.MESH
@@ -365,6 +342,83 @@
     )(att, wo, res, gain, gates, win, wout)
 
 
+def attend_kernel(
+    keys, scale, owners, needed, query, row_prefix, cache, suffix, causal, out, top, total, acc
+):
+    size = suffix.shape[1] // 2
+    heads = query.shape[1] // size
+    tokens = query.shape[0]
+    q = jnp.concatenate([query[:, h * size : (h + 1) * size] for h in range(heads)], axis=0)
+    spot = pl.program_id(0)
+
+    def scores_of(k):
+        return (
+            lax.dot_general(q, k, (((1,), (1,)), ((), ())), preferred_element_type=jnp.float32)
+            * scale
+        )
+
+    @pl.when(spot == 0)
+    def _():
+        seen = jnp.concatenate([causal[...]] * heads, axis=0) > 0.5
+        scores = jnp.where(seen, scores_of(suffix[:, :size]), -jnp.inf)
+        high = jnp.max(scores, axis=1, keepdims=True)
+        weights = jnp.exp(scores - high)
+        top[...] = high
+        total[...] = jnp.sum(weights, axis=1, keepdims=True)
+        acc[...] = jnp.dot(
+            weights.astype(jnp.bfloat16), suffix[:, size:], preferred_element_type=jnp.float32
+        )
+
+    @pl.when(needed[spot] > 0)
+    def _():
+        match = row_prefix[...] == owners[spot]
+        scores = jnp.where(match, scores_of(cache[0, :keys, :size]), -jnp.inf)
+        high = jnp.maximum(top[...], jnp.max(scores, axis=1, keepdims=True))
+        weights = jnp.exp(scores - high)
+        shrink = jnp.exp(top[...] - high)
+        top[...] = high
+        total[...] = total[...] * shrink + jnp.sum(weights, axis=1, keepdims=True)
+        acc[...] = acc[...] * shrink + jnp.dot(
+            weights.astype(jnp.bfloat16),
+            cache[0, :keys, size:],
+            preferred_element_type=jnp.float32,
+        )
+
+    @pl.when(spot == pl.num_programs(0) - 1)
+    def _():
+        result = (acc[...] / total[...]).astype(jnp.bfloat16)
+        for h in range(heads):
+            out[:, h * size : (h + 1) * size] = result[h * tokens : (h + 1) * tokens]
+
+
+def attend(keys, scale, owners, needed, query, row_prefix, cache, suffix, causal):
+    heads = query.shape[1] * 2 // suffix.shape[1]
+    lines = heads * query.shape[0]
+    smem = pl.BlockSpec(memory_space=pltpu.SMEM)
+    vmem = pl.BlockSpec(memory_space=pltpu.VMEM)
+    return pl.pallas_call(
+        functools.partial(attend_kernel, keys, scale),
+        grid=(cache.shape[0],),
+        out_shape=jax.ShapeDtypeStruct(query.shape, jnp.bfloat16),
+        in_specs=[
+            smem,
+            smem,
+            vmem,
+            vmem,
+            pl.BlockSpec((1, cache.shape[1], cache.shape[2]), lambda i: (i, 0, 0)),
+            vmem,
+            vmem,
+        ],
+        out_specs=vmem,
+        scratch_shapes=[
+            pltpu.VMEM((lines, 1), jnp.float32),
+            pltpu.VMEM((lines, 1), jnp.float32),
+            pltpu.VMEM((lines, suffix.shape[1] // 2), jnp.float32),
+        ],
+        compiler_params=pltpu.CompilerParams(vmem_limit_bytes=48 * 2**20),
+    )(owners, needed, query, row_prefix, cache, suffix, causal)
+
+
 def body(
     query,
     suffix_kv,
@@ -385,60 +439,47 @@
     heads_here = query.shape[1] // head_size
     kv_head = lax.axis_index("tensor") * heads_here // (QH // KVH)
     score_scale = head_size ** (-0.5)
-    queries = query.reshape(tok_rows, heads_here, head_size)
     segments = segment_ids[0]
     requests = jnp.arange(request_prefix.shape[1], dtype=jnp.int32)
     row_prefix = jnp.sum(
         jnp.where(segments[:, None] == requests[None, :], request_prefix[0][None, :], 0), axis=1
     )
-    blank_state = (
-        jnp.full((tok_rows, heads_here), NEG_FLOOR, jnp.float32),
-        jnp.zeros((tok_rows, heads_here), jnp.float32),
-        jnp.zeros((tok_rows, heads_here, head_size), jnp.float32),
-    )
     shard_len = prefix_kv.shape[0]
-    own_cache = lax.dynamic_slice_in_dim(prefix_kv, kv_head, 1, 1).reshape(shard_len, 2 * head_size)
-    cache_rows = lax.all_gather(own_cache, "seq", axis=0, tiled=True)
     exp_here = expert_in.shape[0]
     members = lax.axis_size("seq")
     experts = exp_here * members
     named = expert_ids[:, :, None] == jnp.arange(experts, dtype=jnp.int32)[None, None, :]
     gates = jnp.sum(jnp.where(named, gate_weights[:, :, None], 0.0), axis=1)
-    owner_rows = jnp.broadcast_to(shard_prefix.astype(jnp.float32)[:, None], (8, experts))
-    small = lax.all_gather(jnp.concatenate([gates, owner_rows], axis=0), "seq", axis=0)
-    owners = small[:, tok_rows, 0].astype(jnp.int32)
+    gate_rows = gates.astype(jnp.bfloat16).reshape(-1, 2 * head_size)
+    owner_rows = jnp.broadcast_to(shard_prefix.astype(jnp.bfloat16)[:, None], (8, 2 * head_size))
+    own_cache = lax.dynamic_slice_in_dim(prefix_kv, kv_head, 1, 1).reshape(shard_len, 2 * head_size)
+    packed = jnp.concatenate([own_cache, owner_rows, gate_rows], axis=0)
+    cache = lax.all_gather(packed, "seq", axis=0, tiled=True)
+    cache = cache.reshape(members, packed.shape[0], 2 * head_size)
+    owners = cache[:, shard_len, 0].astype(jnp.int32)
+    small = cache[:, shard_len + 8 :].astype(jnp.float32).reshape(members, tok_rows, experts)
     me = lax.axis_index("seq")
-    own_gates = lax.dynamic_slice_in_dim(small[:, :tok_rows], me * exp_here, exp_here, 2)
     index = jnp.arange(members, dtype=jnp.int32)
+    own_gates = lax.dynamic_slice_in_dim(small, me * exp_here, exp_here, 2)
     chosen = (index ^ me)[:, None] == index[None, :]
     own_gates = jnp.sum(jnp.where(chosen[:, :, None, None], own_gates[None], 0.0), axis=1)
     own_gates = own_gates.reshape(members * tok_rows, exp_here)
-    shard_count = owners.shape[0]
-    shards = cache_rows.reshape(shard_count, -1, 2, head_size)
-
-    def one_shard(inner_state, shard_item):
-        block_rows, shard_owner = shard_item
-        matching = row_prefix == shard_owner
-
-        def attend(current):
-            allowed = jnp.broadcast_to(matching[:, None], (tok_rows, block_rows.shape[0]))
-            return fold_block(
-                current, queries, block_rows[:, 0], block_rows[:, 1], allowed, score_scale
-            )
-
-        return (lax.cond(jnp.any(matching), attend, lambda current: current, inner_state), None)
-
-    final_state, unused = lax.scan(one_shard, blank_state, (shards, owners))
-    carried = final_state
-    own_suffix = lax.dynamic_slice_in_dim(suffix_kv, kv_head, 1, 1).reshape(tok_rows, 2, head_size)
+    needed = jnp.any(owners[:, None] == row_prefix[None, :], axis=1).astype(jnp.int32)
+    own_suffix = lax.dynamic_slice_in_dim(suffix_kv, kv_head, 1, 1).reshape(
+        tok_rows, 2 * head_size
+    )
     positions = jnp.arange(tok_rows)
     causal = (segments[:, None] == segments[None, :]) & (positions[None, :] <= positions[:, None])
-    carried = fold_block(carried, queries, own_suffix[:, 0], own_suffix[:, 1], causal, score_scale)
-    running_max, running_sum, weighted = carried
-    attention = (
-        (weighted / running_sum[:, :, None])
-        .reshape(tok_rows, heads_here * head_size)
-        .astype(jnp.bfloat16)
+    attention = attend(
+        shard_len,
+        score_scale,
+        owners,
+        needed,
+        query,
+        jnp.tile(row_prefix[:, None], (heads_here, 1)),
+        cache,
+        own_suffix,
+        causal.astype(jnp.float32),
     )
     slice_width = query.shape[1]
     first_col = lax.axis_index("tensor") * slice_width

time: 239 us -> 201 us (0.84)
  waiting for transfers between devices: 23.6 us -> 59 us
  blocking collectives: 32.8 us -> 0 us
  local copies, waits for them, and re-layouts: 54.8 us -> 27.1 us
  Pallas kernels: 84 us -> 95.6 us
  other arithmetic: 14.7 us -> 4.01 us
  matrix products: 8.89 us -> 0 us
  loops' own time: 6.04 us -> 0 us
    all_gather x1, waiting for transfers between devices: 23.5 us -> 59 us  [body(): cache = lax.all_gather(packed, 'seq', axis=0, tiled=True)]
    all_gather x1 -> x0, blocking collectives: 32.8 us -> none  [body(): lax.all_gather(jnp.concatenate([gates, owner_rows], axis=0), 'seq', axis=0)]
    pallas_call x0 -> x1, Pallas kernels: none -> 11.3 us  [attend(): pl.pallas_call(functools.partial(attend_kernel, keys, scale), grid=(cache...]
    reduce_or x8 -> x1, other arithmetic: 10.4 us -> 0.18 us  [body(): jnp.any(owners[:, None] == row_prefix[None, :], axis=1).astype(jnp.int32)]
    dot_general x18 -> x0, matrix products: 8.89 us -> none  [the longest x9 5.13 us: fold_block(): jnp.einsum('rhk,kd->rhd', weights.astype(jnp.bfloat16), values, preferred...]
    squeeze x8 -> x0, local copies, waits for them, and re-layouts: 8.67 us -> none  [body(): final_state, unused = lax.scan(one_shard, blank_state, (shards, owners))]
    unnamed x19 -> x17, local copies, waits for them, and re-layouts: 19.5 us -> 12.3 us
    while x3 -> x0, local copies, waits for them, and re-layouts: 6.9 us -> none  [body(): final_state, unused = lax.scan(one_shard, blank_state, (shards, owners))]
  transfers between devices with their start and end apart: 1 -> 1, of which waited for: 1 -> 1; matrix products, arithmetic and copies ran while one was open for 8% -> 9% of each run, Pallas kernels for 0% -> 0%
where the time goes in v3:
time: 201 us
  Pallas kernels  95.6 us (48%)
  waiting for transfers between devices  59 us (29%)
  local copies, waits for them, and re-layouts  27.1 us (13%)
  between operations  14.9 us (7%)
  other arithmetic  4.01 us (2%)
    pallas_call x1, Pallas kernels, moe(): pl.pallas_call(functools.partial(moe_kernel, ns, nt), out_shape=[jax.Shap...  84.3 us
    all_gather x1, waiting for transfers between devices, body(): cache = lax.all_gather(packed, 'seq', axis=0, tiled=True)  59 us
    unnamed x17, local copies, waits for them, and re-layouts  12.3 us
    pallas_call x1, Pallas kernels, attend(): pl.pallas_call(functools.partial(attend_kernel, keys, scale), grid=(cache...  11.3 us
    reshape x1, local copies, waits for them, and re-layouts, body(): jnp.transpose(expert_in, (2, 1, 0, 3)).reshape(2, expert_in.shape[1], width)  8.49 us
  transfers between devices with their start and end apart: 1, of which 1 were waited for; matrix products, arithmetic and copies ran while one was open for 9% of the time, Pallas kernels for 0%

profile of v3, /device:TPU:0, one launch (start us, length us, event | category | flops | bytes accessed | tf_op | source)
XLA Modules:
  0.0 200.7 jit_solution(13803577356853835539)
XLA Ops:
  7.2 0.0 copy-start
  7.2 0.0 copy-start.5
  7.2 0.0 copy-start.4
  7.2 0.0 all-gather.2.cloned.1.call-start
  8.0 0.7 select_reduce_fusion.1
  8.7 0.1 copy.23
  8.8 0.1 convert_element_type.24
  8.9 1.4 constant_dynamic-slice_fusion.3
  10.3 0.1 copy.33
  10.4 1.0 pad_maximum_fusion
  11.5 0.0 all-gather.2.cloned.1.call-update
  11.5 0.9 constant_dynamic-slice_fusion.2
  12.4 0.0 copy-done.5
  12.4 0.0 copy-done.4
  12.4 0.1 select_reduce_fusion.2
  12.5 0.1 copy.24.row_prefix
  12.7 6.2 %copy.27 = bf16[2,2048,2,352]{1,3,0,2:T(8,128)(2,1)} copy(bf16[2,2048,2,352]{1,3,2,0:T(8,128)(2,1)} %param.24) | data formatting | bytes 11534336 | tf_op args[11]
  18.8 8.5 %copy.28.win_hbm = bf16[2,2048,704]{2,1,0:T(8,128)(2,1)} copy(bf16[2,2048,704]{1,2,0:T(8,128)(2,1)} %bitcast.25) | data formatting | bytes 11534336 | tf_op jit(solution)/shard_map/reshape | solution.py:487
  27.3 0.0 copy-start.3
  27.3 1.4 dynamic_slice.18
  28.7 0.0 copy-done
  28.7 0.7 constant_dynamic-slice_fusion.1.res
  29.4 0.1 iota_compare_fusion.2
  29.5 0.1 fusion.1.causal
  29.6 59.0 %all-gather.2.cloned.1.call-done = bf16[8320,256]{1,0:T(8,128)(2,1)} async-done(((bf16[1040,256]{1,0:T(8,128)(2,1)}), bf16[8320,256]{1,0:T(8,128)(2,1)}) %all-gather.2.cloned.1.call-update) | async-done | bytes 4259856 | tf_op jit(solution)/shard_map/all_gather | solution.py:457
  88.5 1.0 fusion.2.owners
  89.5 0.8 slice_convert_fusion
  90.3 0.2 compare_reduce_fusion
  90.5 0.2 reshape.84
  90.7 0.2 constant_dynamic-slice_fusion
  90.9 0.2 copy.25
  91.0 0.1 select_reduce_fusion
  91.2 1.0 copy.26
  92.2 0.0 copy-done.3
  92.2 0.0 copy-start.1
  92.2 2.2 %copy-done.1 = bf16[8320,256]{1,0:T(8,128)(2,1)S(1)} copy-done((bf16[8320,256]{1,0:T(8,128)(2,1)S(1)}, bf16[8320,256]{1,0:T(8,128)(2,1)}, u32[]{:S(2)}) %copy-start.1) | copy-done | bytes 4259864
  94.4 11.3 %shard_map.140.att = bf16[128,512]{1,0:T(8,128)(2,1)S(1)} custom-call(s32[8]{0:T(128)S(1)} %fusion.2.owners, s32[8]{0:T(128)S(1)} %convert_element_type.27.needed, bf16[128,512]{1,0:T(8,128)(2,1)S(1)} %copy-done.3, s32[512,1]{1,0:T(8,128)S(1)} %copy.24.row_prefix, bf16[8,1040,256]{2,1,0:T(8,128)(2,1)S(1)} %bitcast.23, bf16[128,256]{1,0:T(8,128)(2,1)S(1)} %bitcast.24, ...), custom_call_target="tpu_custom_call" | custom-call | tf_op jit(solution)/shard_map/pallas_call | solution.py:399
  105.7 0.0 copy-start.2
  105.7 0.6 copy-done.2
  106.4 84.3 %shard_map.141 = (bf16[128,512]{1,0:T(8,128)(2,1)}, bf16[128,512]{1,0:T(8,128)(2,1)}) custom-call(bf16[128,512]{1,0:T(8,128)(2,1)} %copy-done.2, bf16[512,2048]{1,0:T(8,128)(2,1)} %wo.1, bf16[128,512]{1,0:T(8,128)(2,1)} %constant_dynamic-slice_fusion.1.res, f32[1,512]{1,0:T(1,128)} %bitcast.32, f32[1024,2]{1,0:T(8,128)} %bitcast.27, ...), custom_call_target="tpu_custom_call" | custom-call | tf_op jit(solution)/shard_map/pallas_call | solution.py:333
  190.7 1.6 copy.38
  192.3 1.6 copy.39
  (6 shorter events, 0.0 us)
Async XLA Ops:
  7.2 21.6 %copy-start = (bf16[128,2048]{1,0:T(8,128)(2,1)S(1)}, bf16[128,2048]{1,0:T(8,128)(2,1)}, u32[]{:S(2)}) copy-start(bf16[128,2048]{1,0:T(8,128)(2,1)} %param.19) | copy-start | bytes 1572868
  7.2 5.2 %copy-start.5 = (s32[1,4]{1,0:T(1,128)S(1)}, s32[1,4]{1,0:T(1,128)}, u32[]{:S(2)}) copy-start(s32[1,4]{1,0:T(1,128)} %param.16) | copy-start | bytes 52
  7.2 5.2 %copy-start.4 = (s32[1,128]{1,0:T(1,128)S(1)}, s32[1,128]{1,0:T(1,128)}, u32[]{:S(2)}) copy-start(s32[1,128]{1,0:T(1,128)} %param.15) | copy-start | bytes 1540
  7.2 81.3 %all-gather.2.cloned.1.call-start = ((), (), s32[]{:S(2)}) async-start(), calls=%async_computation | async-start | bytes 4792320 | tf_op jit(solution)/shard_map/all_gather | solution.py:457
  27.3 64.9 %copy-start.3 = (bf16[128,512]{1,0:T(8,128)(2,1)S(1)}, bf16[128,512]{1,0:T(8,128)(2,1)}, u32[]{:S(2)}) copy-start(bf16[128,512]{1,0:T(8,128)(2,1)} %query.1) | copy-start | bytes 393220
  92.2 2.2 %copy-start.1 = (bf16[8320,256]{1,0:T(8,128)(2,1)S(1)}, bf16[8320,256]{1,0:T(8,128)(2,1)}, u32[]{:S(2)}) copy-start(bf16[8320,256]{1,0:T(8,128)(2,1)} %all-gather.2.cloned.1.call-done) | copy-start | bytes 12779524
  105.7 0.7 copy-start.2
Sparse Core Ops, SparseCore 0:
  11.6 76.8 all-gather.1
